TPU v7x, 32 devices: a whole 2x2x4 slice. The times are simulated.
32 devices in a mesh: dp: 8 (over z, x), tensor: 4 (over y, core).
Axes of the slice: x: 2, y: 2, z: 4, core: 2. Of those that a mesh axis runs over, the one named last changes fastest.
Arguments:
- tokens: bfloat16 [32768, 256], P('dp'), may hold values from -6 to 6
- positions: bfloat16 [32768, 256], P('dp'), may hold values from -1 to 1
- segment_ids: int32 [8, 4096], P('dp'), may hold values from 0 to 4, as said below
- pad_flags: int32 [8, 4096], P('dp'), may hold values from 0 to 1, as said below
- cotangent: bfloat16 [32768, 256], P('dp'), may hold values from -6 to 6
- inward: float32 [3, 256, 256], P(None, 'dp', 'tensor'), may hold values from -0.375 to 0.375
- outward: float32 [256, 256], P('tensor', 'dp'), may hold values from -1 to 1
- upward: float32 [256, 2048], P('dp', 'tensor'), may hold values from -0.375 to 0.375
- downward: float32 [2048, 256], P('tensor', 'dp'), may hold values from -0.1875 to 0.1875
- vectors: float32 [6, 256], P(None, 'dp')
- offsets: float32 [2, 256], P(None, ('tensor', 'dp')), may hold values from -4 to 4
- shifts: float32 [2048], P(('tensor', 'dp')), may hold values from -4 to 4
- first_inward: float32 [3, 256, 256], P(None, 'dp', 'tensor'), may hold values from -1536 to 1536
- first_outward: float32 [256, 256], P('tensor', 'dp'), may hold values from -224 to 224
- first_upward: float32 [256, 2048], P('dp', 'tensor'), may hold values from -224 to 224
- first_downward: float32 [2048, 256], P('tensor', 'dp'), may hold values from -512 to 512
- first_vectors: float32 [6, 256], P(None, 'dp'), may hold values from -768 to 768
- first_offsets: float32 [2, 256], P(None, ('tensor', 'dp')), may hold values from -1536 to 1536
- first_shifts: float32 [2048], P(('tensor', 'dp')), may hold values from -224 to 224
- second_inward: float32 [3, 256, 256], P(None, 'dp', 'tensor'), may hold values from 73728 to 294912
- second_outward: float32 [256, 256], P('tensor', 'dp'), may hold values from 1310.72 to 5242.88
- second_upward: float32 [256, 2048], P('dp', 'tensor'), may hold values from 1310.72 to 5242.88
- second_downward: float32 [2048, 256], P('tensor', 'dp'), may hold values from 6553.6 to 26214.4
- second_vectors: float32 [6, 256], P(None, 'dp'), may hold values from 16384 to 65536
- second_offsets: float32 [2, 256], P(None, ('tensor', 'dp')), may hold values from 73728 to 294912
- second_shifts: float32 [2048], P(('tensor', 'dp')), may hold values from 1310.72 to 5242.88
Outputs:
- encoded: bfloat16 [32768, 256], P('dp')
- token_grad: float32 [32768, 256], P('dp')
- grad_inward: float32 [3, 256, 256], P(None, 'dp', 'tensor')
- grad_outward: float32 [256, 256], P('tensor', 'dp')
- grad_upward: float32 [256, 2048], P('dp', 'tensor')
- grad_downward: float32 [2048, 256], P('tensor', 'dp')
- grad_vectors: float32 [6, 256], P(None, 'dp')
- grad_offsets: float32 [2, 256], P(None, ('tensor', 'dp'))
- grad_shifts: float32 [2048], P(('tensor', 'dp'))
- updated_inward: float32 [3, 256, 256], P(None, 'dp', 'tensor')
- updated_outward: float32 [256, 256], P('tensor', 'dp')
- updated_upward: float32 [256, 2048], P('dp', 'tensor')
- updated_downward: float32 [2048, 256], P('tensor', 'dp')
- updated_vectors: float32 [6, 256], P(None, 'dp')
- updated_offsets: float32 [2, 256], P(None, ('tensor', 'dp'))
- updated_shifts: float32 [2048], P(('tensor', 'dp'))
- lowered_inward: bfloat16 [3, 256, 256], P(None, 'dp', 'tensor')
- lowered_outward: bfloat16 [256, 256], P('tensor', 'dp')
- lowered_upward: bfloat16 [256, 2048], P('dp', 'tensor')
- lowered_downward: bfloat16 [2048, 256], P('tensor', 'dp')
- momentum_inward: float32 [3, 256, 256], P(None, 'dp', 'tensor')
- momentum_outward: float32 [256, 256], P('tensor', 'dp')
- momentum_upward: float32 [256, 2048], P('dp', 'tensor')
- momentum_downward: float32 [2048, 256], P('tensor', 'dp')
- momentum_vectors: float32 [6, 256], P(None, 'dp')
- momentum_offsets: float32 [2, 256], P(None, ('tensor', 'dp'))
- momentum_shifts: float32 [2048], P(('tensor', 'dp'))
- variance_inward: float32 [3, 256, 256], P(None, 'dp', 'tensor')
- variance_outward: float32 [256, 256], P('tensor', 'dp')
- variance_upward: float32 [256, 2048], P('dp', 'tensor')
- variance_downward: float32 [2048, 256], P('tensor', 'dp')
- variance_vectors: float32 [6, 256], P(None, 'dp')
- variance_offsets: float32 [2, 256], P(None, ('tensor', 'dp'))
- variance_shifts: float32 [2048], P(('tensor', 'dp'))
Inputs may be any that keep to these rules, and one draw needn't show every extreme that they name: `segment_ids`: in every pack the ids never fall and every id from 0 to 4 occurs. `pad_flags`: the first token of every image is never padding.
All inputs are finite; a program needn't handle non-finite values.
Results may differ from a plain program's by a relative error of at most 0.008.
The roundings to bfloat16 on the way count: a program that leaves them out, or rounds other values in their place, can miss the bound.
Values may be sent and summed in bfloat16 or wider, within the bound.
A program may use at most 128 MiB of HBM per device.

v0:
```python
import jax
import jax.numpy as jnp
from jax import lax
from jax.sharding import PartitionSpec as P

HEAD_DIM = 32
STEP = 10
neg_fill = -1e30
norm_eps = 1e-05
beta_one = 0.5
beta_two = 0.5
adam_eps = 1e-08
decay_rate = 0.0001
step_rates = (0.06, 0.15, 0.06, 0.03, 0.1, 0.1, 0.1)
block_limit = 512


def product(left_side, right_side):
    return jnp.dot(left_side, right_side, preferred_element_type=jnp.float32)


def product_left(left_side, right_side):
    return lax.dot_general(
        left_side, right_side, (((0,), (0,)), ((), ())), preferred_element_type=jnp.float32
    )


def product_right(left_side, right_side):
    return lax.dot_general(
        left_side, right_side, (((1,), (1,)), ((), ())), preferred_element_type=jnp.float32
    )


def smooth_unit(values):
    return jax.nn.gelu(values, approximate=False)


def norm_forward(values, gain_row, shift_row):
    center = values - jnp.mean(values, axis=-1, keepdims=True)
    inverse = lax.rsqrt(jnp.mean(center * center, axis=-1, keepdims=True) + norm_eps)
    scaled = center * inverse
    return (scaled * gain_row + shift_row, scaled, inverse)


def norm_backward(upstream, scaled, inverse, gain_row):
    spread = upstream * gain_row
    centred = (
        spread
        - jnp.mean(spread, axis=-1, keepdims=True)
        - scaled * jnp.mean(spread * scaled, axis=-1, keepdims=True)
    )
    return (inverse * centred, jnp.sum(upstream * scaled, axis=0), jnp.sum(upstream, axis=0))


def summed(partial_value):
    return lax.psum(partial_value, "tensor")


def mask_scores(query_block, key_heads, seg_block, segment, key_open):
    scores = jnp.einsum(
        "qhd,khd->hqk", query_block, key_heads, preferred_element_type=jnp.float32
    ) * HEAD_DIM ** (-0.5)
    allowed = (seg_block[:, None] == segment[None, :]) & key_open[None, :]
    return jnp.where(allowed[None], scores, neg_fill)


def attend_forward(queries, key_rows, values, segment, key_open):
    row_count = queries.shape[0]
    block_rows = min(block_limit, row_count)
    heads_here = queries.shape[1] // HEAD_DIM
    key_heads = key_rows.reshape(row_count, heads_here, HEAD_DIM)
    value_heads = values.reshape(row_count, heads_here, HEAD_DIM)

    def one_block(block_index):
        first_row = block_index * block_rows
        query_block = lax.dynamic_slice_in_dim(queries, first_row, block_rows, 0).reshape(
            block_rows, heads_here, HEAD_DIM
        )
        seg_block = lax.dynamic_slice_in_dim(segment, first_row, block_rows, 0)
        scores = mask_scores(query_block, key_heads, seg_block, segment, key_open)
        maxima = jnp.max(scores, axis=-1, keepdims=True)
        exponent = jnp.exp(scores - maxima)
        totals = jnp.sum(exponent, axis=-1, keepdims=True)
        weights = (exponent / totals).astype(jnp.bfloat16)
        context = jnp.einsum(
            "hqk,khd->qhd", weights, value_heads, preferred_element_type=jnp.float32
        )
        return (
            context.reshape(block_rows, heads_here * HEAD_DIM),
            (maxima + jnp.log(totals))[:, :, 0],
        )

    contexts, log_totals = lax.map(one_block, jnp.arange(row_count // block_rows))
    return (contexts.reshape(row_count, heads_here * HEAD_DIM), log_totals)


def attend_backward(queries, key_rows, values, segment, key_open, log_totals, context_grad):
    row_count = queries.shape[0]
    block_rows = min(block_limit, row_count)
    heads_here = queries.shape[1] // HEAD_DIM
    key_heads = key_rows.reshape(row_count, heads_here, HEAD_DIM)
    value_heads = values.reshape(row_count, heads_here, HEAD_DIM)
    scale_value = HEAD_DIM ** (-0.5)

    def one_block(carry, block_index):
        key_total, value_total = carry
        first_row = block_index * block_rows
        query_block = lax.dynamic_slice_in_dim(queries, first_row, block_rows, 0).reshape(
            block_rows, heads_here, HEAD_DIM
        )
        grad_block = lax.dynamic_slice_in_dim(context_grad, first_row, block_rows, 0).reshape(
            block_rows, heads_here, HEAD_DIM
        )
        seg_block = lax.dynamic_slice_in_dim(segment, first_row, block_rows, 0)
        scores = mask_scores(query_block, key_heads, seg_block, segment, key_open)
        probs = jnp.exp(scores - log_totals[block_index][:, :, None])
        prob_grad = jnp.einsum(
            "qhd,khd->hqk", grad_block, value_heads, preferred_element_type=jnp.float32
        )
        delta = jnp.sum(probs * prob_grad, axis=-1, keepdims=True)
        score_grad = (probs * (prob_grad - delta)).astype(jnp.bfloat16)
        query_grad = (
            jnp.einsum("hqk,khd->qhd", score_grad, key_heads, preferred_element_type=jnp.float32)
            * scale_value
        )
        key_total = key_total + jnp.einsum(
            "hqk,qhd->khd", score_grad, query_block, preferred_element_type=jnp.float32
        )
        value_total = value_total + jnp.einsum(
            "hqk,qhd->khd",
            probs.astype(jnp.bfloat16),
            grad_block,
            preferred_element_type=jnp.float32,
        )
        return (
            (key_total, value_total),
            query_grad.astype(jnp.bfloat16).reshape(block_rows, heads_here * HEAD_DIM),
        )

    zeros_init = jnp.zeros((row_count, heads_here, HEAD_DIM), jnp.float32)
    (key_total, value_total), query_grads = lax.scan(
        one_block, (zeros_init, zeros_init), jnp.arange(row_count // block_rows)
    )
    query_grad = query_grads.reshape(row_count, heads_here * HEAD_DIM)
    key_grad = (
        (key_total * scale_value).astype(jnp.bfloat16).reshape(row_count, heads_here * HEAD_DIM)
    )
    value_grad = value_total.astype(jnp.bfloat16).reshape(row_count, heads_here * HEAD_DIM)
    return (query_grad, key_grad, value_grad)


def adamw(master, gradient, old_first, old_second, step_rate):
    momentum = beta_one * old_first + (1.0 - beta_one) * gradient
    variance = beta_two * old_second + (1.0 - beta_two) * gradient * gradient
    normal_step = (
        momentum / (1.0 - beta_one**STEP) / (jnp.sqrt(variance / (1.0 - beta_two**STEP)) + adam_eps)
    )
    return (master - step_rate * (normal_step + decay_rate * master), momentum, variance)


def body(
    tokens,
    positions,
    segment_ids,
    pad_flags,
    cotangent,
    inward,
    outward,
    upward,
    downward,
    vectors,
    offsets,
    shifts,
    first_inward,
    first_outward,
    first_upward,
    first_downward,
    first_vectors,
    first_offsets,
    first_shifts,
    second_inward,
    second_outward,
    second_upward,
    second_downward,
    second_vectors,
    second_offsets,
    second_shifts,
):
    w_inward, w_outward, w_upward, w_downward, vector_low, offset_low, shift_low = (
        lax.all_gather(inward.astype(jnp.bfloat16), "dp", axis=1, tiled=True),
        lax.all_gather(outward.astype(jnp.bfloat16), "dp", axis=1, tiled=True),
        lax.all_gather(upward.astype(jnp.bfloat16), "dp", axis=0, tiled=True),
        lax.all_gather(downward.astype(jnp.bfloat16), "dp", axis=1, tiled=True),
        lax.all_gather(vectors.astype(jnp.bfloat16), "dp", axis=1, tiled=True),
        lax.all_gather(offsets.astype(jnp.bfloat16), "dp", axis=1, tiled=True),
        lax.all_gather(shifts.astype(jnp.bfloat16), "dp", axis=0, tiled=True),
    )
    vector_wide = vector_low.astype(jnp.float32)
    offset_wide = offset_low.astype(jnp.float32)
    shift_wide = shift_low.astype(jnp.float32)
    segment = segment_ids[0]
    key_open = pad_flags[0] == 0
    input_wide = tokens.astype(jnp.float32)
    query_in = (input_wide + positions.astype(jnp.float32)).astype(jnp.bfloat16)
    queries = (product(query_in, w_inward[0]) + offset_wide[0]).astype(jnp.bfloat16)
    key_rows = product(query_in, w_inward[1]).astype(jnp.bfloat16)
    values = (product(tokens, w_inward[2]) + offset_wide[1]).astype(jnp.bfloat16)
    context, log_totals = attend_forward(queries, key_rows, values, segment, key_open)
    context_low = context.astype(jnp.bfloat16)
    first_sum = input_wide + summed(product(context_low, w_outward)) + vector_wide[4]
    normed, scaled_one, inverse_one = norm_forward(first_sum, vector_wide[0], vector_wide[1])
    normed_low = normed.astype(jnp.bfloat16)
    hidden = product(normed_low, w_upward) + shift_wide
    unit_value, unit_back = jax.vjp(smooth_unit, hidden)
    active = unit_value.astype(jnp.bfloat16)
    second_sum = normed + summed(product(active, w_downward)) + vector_wide[5]
    result, scaled_two, inverse_two = norm_forward(second_sum, vector_wide[2], vector_wide[3])
    encoded = result.astype(jnp.bfloat16)
    upstream = cotangent.astype(jnp.float32)
    second_grad, gain_two, shift_two = norm_backward(
        upstream, scaled_two, inverse_two, vector_wide[2]
    )
    down_low = second_grad.astype(jnp.bfloat16)
    grad_downward = product_left(active, down_low)
    hidden_low = unit_back(product_right(down_low, w_downward))[0].astype(jnp.bfloat16)
    grad_upward = product_left(normed_low, hidden_low)
    grad_shifts = jnp.sum(hidden_low.astype(jnp.float32), axis=0)
    normed_grad = second_grad + summed(product_right(hidden_low, w_upward))
    first_grad, gain_one, shift_one = norm_backward(
        normed_grad, scaled_one, inverse_one, vector_wide[0]
    )
    first_low = first_grad.astype(jnp.bfloat16)
    grad_outward = product_left(context_low, first_low)
    context_grad = product_right(first_low, w_outward).astype(jnp.bfloat16)
    query_grad, key_grad, value_grad = attend_backward(
        queries, key_rows, values, segment, key_open, log_totals, context_grad
    )
    grad_inward = jnp.stack(
        [
            product_left(query_in, query_grad),
            product_left(query_in, key_grad),
            product_left(tokens, value_grad),
        ]
    )
    grad_offsets = jnp.stack(
        [
            jnp.sum(query_grad.astype(jnp.float32), axis=0),
            jnp.sum(value_grad.astype(jnp.float32), axis=0),
        ]
    )
    input_part = (
        product_right(query_grad, w_inward[0])
        + product_right(key_grad, w_inward[1])
        + product_right(value_grad, w_inward[2])
    )
    input_grad = first_grad + summed(input_part)
    grad_vectors = jnp.stack(
        [
            gain_one,
            shift_one,
            gain_two,
            shift_two,
            jnp.sum(first_grad, axis=0),
            jnp.sum(second_grad, axis=0),
        ]
    )
    reduced = (
        lax.psum_scatter(grad_inward, "dp", scatter_dimension=1, tiled=True),
        lax.psum_scatter(grad_outward, "dp", scatter_dimension=1, tiled=True),
        lax.psum_scatter(grad_upward, "dp", scatter_dimension=0, tiled=True),
        lax.psum_scatter(grad_downward, "dp", scatter_dimension=1, tiled=True),
        lax.psum_scatter(grad_vectors, "dp", scatter_dimension=1, tiled=True),
        lax.psum_scatter(grad_offsets, "dp", scatter_dimension=1, tiled=True),
        lax.psum_scatter(grad_shifts, "dp", scatter_dimension=0, tiled=True),
    )
    masters = (inward, outward, upward, downward, vectors, offsets, shifts)
    firsts = (
        first_inward,
        first_outward,
        first_upward,
        first_downward,
        first_vectors,
        first_offsets,
        first_shifts,
    )
    seconds = (
        second_inward,
        second_outward,
        second_upward,
        second_downward,
        second_vectors,
        second_offsets,
        second_shifts,
    )
    updated = []
    momenta = []
    variances = []
    for master, gradient, old_first, old_second, step_rate in zip(
        masters, reduced, firsts, seconds, step_rates
    ):
        new_master, momentum, variance = adamw(master, gradient, old_first, old_second, step_rate)
        updated.append(new_master)
        momenta.append(momentum)
        variances.append(variance)
    return (
        encoded,
        input_grad,
        reduced[0],
        reduced[1],
        reduced[2],
        reduced[3],
        reduced[4],
        reduced[5],
        reduced[6],
        updated[0],
        updated[1],
        updated[2],
        updated[3],
        updated[4],
        updated[5],
        updated[6],
        updated[0].astype(jnp.bfloat16),
        updated[1].astype(jnp.bfloat16),
        updated[2].astype(jnp.bfloat16),
        updated[3].astype(jnp.bfloat16),
        momenta[0],
        momenta[1],
        momenta[2],
        momenta[3],
        momenta[4],
        momenta[5],
        momenta[6],
        variances[0],
        variances[1],
        variances[2],
        variances[3],
        variances[4],
        variances[5],
        variances[6],
    )


def solution(mesh):
    in_specs = (
        P("dp", None),
        P("dp", None),
        P("dp", None),
        P("dp", None),
        P("dp", None),
        P(None, "dp", "tensor"),
        P("tensor", "dp"),
        P("dp", "tensor"),
        P("tensor", "dp"),
        P(None, "dp"),
        P(None, ("tensor", "dp")),
        P(("tensor", "dp")),
        P(None, "dp", "tensor"),
        P("tensor", "dp"),
        P("dp", "tensor"),
        P("tensor", "dp"),
        P(None, "dp"),
        P(None, ("tensor", "dp")),
        P(("tensor", "dp")),
        P(None, "dp", "tensor"),
        P("tensor", "dp"),
        P("dp", "tensor"),
        P("tensor", "dp"),
        P(None, "dp"),
        P(None, ("tensor", "dp")),
        P(("tensor", "dp")),
    )
    out_specs = (
        P("dp", None),
        P("dp", None),
        P(None, "dp", "tensor"),
        P("tensor", "dp"),
        P("dp", "tensor"),
        P("tensor", "dp"),
        P(None, "dp"),
        P(None, ("tensor", "dp")),
        P(("tensor", "dp")),
        P(None, "dp", "tensor"),
        P("tensor", "dp"),
        P("dp", "tensor"),
        P("tensor", "dp"),
        P(None, "dp"),
        P(None, ("tensor", "dp")),
        P(("tensor", "dp")),
        P(None, "dp", "tensor"),
        P("tensor", "dp"),
        P("dp", "tensor"),
        P("tensor", "dp"),
        P(None, "dp", "tensor"),
        P("tensor", "dp"),
        P("dp", "tensor"),
        P("tensor", "dp"),
        P(None, "dp"),
        P(None, ("tensor", "dp")),
        P(("tensor", "dp")),
        P(None, "dp", "tensor"),
        P("tensor", "dp"),
        P("dp", "tensor"),
        P("tensor", "dp"),
        P(None, "dp"),
        P(None, ("tensor", "dp")),
        P(("tensor", "dp")),
    )
    return jax.shard_map(body, mesh=mesh, in_specs=in_specs, out_specs=out_specs, check_vma=False)
```

profile of v0, /device:TPU:0, one launch (start us, length us, event | category | flops | bytes accessed | tf_op | source)
XLA Modules:
  0.0 1405.3 jit_solution(3010460021737112204)
XLA Ops:
  8.1 22.1 %all-gather = bf16[8,8,2]{1,2,0:T(2,128)(2,1)S(1)} all-gather(bf16[1,8,2]{1,2,0:T(2,128)(2,1)S(1)} %convert_bitcast_fusion.2), channel_id=1, replica_groups=mesh['dp'=8,'tensor'=4] {'dp'}, dimensions={0}, use_global_device_ids=true | all-gather | bytes 288 | tf_op jit(solution)/shard_map/all_gather | solution.py:195
  32.6 32.5 %all_gather.23 = bf16[64,256]{0,1:T(8,128)(2,1)} all-gather(bf16[64,32]{0,1:T(8,128)(2,1)S(1)} %convert_element_type.133), channel_id=1, replica_groups=mesh['dp'=8,'tensor'=4] {'dp'}, dimensions={1}, use_global_device_ids=true | all-gather | bytes 36864 | tf_op jit(solution)/shard_map/all_gather | solution.py:191
  65.1 30.6 %all_gather.21 = bf16[3,256,64]{2,1,0:T(8,128)(2,1)S(1)} all-gather(bf16[3,32,64]{2,1,0:T(8,128)(2,1)S(1)} %convert_element_type.125), channel_id=1, replica_groups=mesh['dp'=8,'tensor'=4] {'dp'}, dimensions={1}, use_global_device_ids=true | all-gather | bytes 110592 | tf_op jit(solution)/shard_map/all_gather | solution.py:190
  101.7 152.2 %while.27 = (s32[]{:T(128)}, bf16[8,512,64]{1,2,0:T(8,128)(2,1)S(1)}, f32[8,2,512]{2,1,0:T(2,128)}, s32[8]{0:T(128)S(1)}, s32[4096]{0:T(1024)}, /*index=5*/s32[1...) while((s32[]{:T(128)}, ...), condition=%wide.region_3.4_spmd, body=%wide.region_0.3_spmd.sunk | while | flops 591395840 | bytes 60221656 | solution.py:93
  259.9 17.4 %all-reduce = bf16[512]{0:T(512)(128)(2,1)S(1)} all-reduce(bf16[512]{0:T(512)(128)(2,1)S(1)} %dynamic-update-slice), channel_id=1, replica_groups=mesh['dp'=8,'tensor'=4] {'dp'}, use_global_device_ids=true, to_apply=%add | all-reduce | flops 512 | bytes 2048
  277.3 26.0 %all-gather.1 = bf16[8,32,6]{1,2,0:T(8,128)(2,1)S(1)} all-gather(bf16[1,32,6]{1,2,0:T(8,128)(2,1)S(1)} %convert_bitcast_fusion.1), channel_id=1, replica_groups=mesh['dp'=8,'tensor'=4] {'dp'}, dimensions={0}, use_global_device_ids=true | all-gather | bytes 3456 | tf_op jit(solution)/shard_map/all_gather | solution.py:194
  303.4 30.8 %all_gather.27 = bf16[512,256]{0,1:T(8,128)(2,1)S(1)} all-gather(bf16[512,32]{0,1:T(8,128)(2,1)S(1)} %convert_element_type.141), channel_id=1, replica_groups=mesh['dp'=8,'tensor'=4] {'dp'}, dimensions={1}, use_global_device_ids=true | all-gather | bytes 294912 | tf_op jit(solution)/shard_map/all_gather | solution.py:193
  334.2 30.7 %all_gather.25 = bf16[256,512]{1,0:T(8,128)(2,1)S(1)} all-gather(bf16[32,512]{1,0:T(8,128)(2,1)S(1)} %convert_element_type.137), channel_id=1, replica_groups=mesh['dp'=8,'tensor'=4] {'dp'}, dimensions={0}, use_global_device_ids=true | all-gather | bytes 294912 | tf_op jit(solution)/shard_map/all_gather | solution.py:192
  371.5 21.6 %multiply_convert_fusion.1 = (bf16[4096,512]{1,0:T(8,128)(2,1)S(1)}, f32[4096,512]{1,0:T(8,128)}, f32[4096,512]{1,0:T(8,128)}) fusion(f32[512]{0:T(512)S(1)} %convert_element_type.139, bf16[4096,256]{1,0:T(8,128)(2,1)S(1)} %fusion.36, bf16[256,512]{1,0:T(8,128)(2,1)S(1)} %all_gather.25), kind=kOutput, calls=%fused_computation.35 | convolution fusion | flops 1212153856 | bytes 23332864 | tf_op jit(solution)/shard_map/dot_general | solution.py:19
  398.5 82.9 %all-reduce.13.cloned.1.call-done = f32[4096,256]{1,0:T(8,128)} async-done(((f32[4096,256]{1,0:T(8,128)}), f32[4096,256]{1,0:T(8,128)}) %all-reduce.13.cloned.1.call-update) | async-done | bytes 4194320 | tf_op jit(solution)/shard_map/psum | solution.py:56
  496.1 8.6 convert_reduce_fusion
  520.9 74.9 %all-reduce.15.cloned.1.call-done = f32[4096,256]{1,0:T(8,128)} async-done(((f32[4096,256]{1,0:T(8,128)}), f32[4096,256]{1,0:T(8,128)}) %all-reduce.15.cloned.1.call-update) | async-done | bytes 4194320 | tf_op jit(solution)/shard_map/psum | solution.py:56
  595.8 6.7 multiply_reduce_fusion.1
  609.9 477.1 %while.28 = (s32[]{:T(128)}, f32[4096,2,32]{0,2,1:T(8,128)S(1)}, f32[4096,2,32]{0,2,1:T(8,128)}, bf16[8,512,64]{1,2,0:T(8,128)(2,1)}, s32[8]{0:T(128)S(1)}, /*in...) while((s32[]{:T(128)}, f32[4096,2,32]{0,2,1:T(8,128)S(1)}, ...), condition=%wide.region_17.18_spmd.clone, body=%wide.region_15.17_spmd.clone.sunk | while | flops 1410399232 | bytes 220977600 | solution.py:141
  623.6 5.7 copy-done
  629.3 7.7 fusion.152
  637.0 15.4 %multiply_reduce_fusion.7 = (f32[2,512]{1,0:T(2,128)S(1)}, f32[2,512,4096]{2,1,0:T(8,128)}) fusion(f32[2,512,4096]{2,1,0:T(8,128)} %copy-done, f32[2,512]{1,0:T(2,128)S(1)} %dynamic-slice_bitcast_fusion.2, pred[512,4096]{1,0:T(8,128)(4,1)} %compare_and_fusion.5, bf16[512,2,32]{0,2,1:T(8,128)(2,1)} %bitcast.191, ...), kind=kOutput, calls=%fused_computation.13.clone.1 | convolution fusion | flops 289405952 | bytes 36249600 | tf_op jit(solution)/shard_map/while/body/eval_jaxpr/qhd,khd->hqk/dot_general | solution.py:117
  652.4 12.5 multiply_convert_fusion.4
  688.7 8.0 fusion.152
  696.7 15.4 %multiply_reduce_fusion.7 = (f32[2,512]{1,0:T(2,128)S(1)}, f32[2,512,4096]{2,1,0:T(8,128)}) fusion(f32[2,512,4096]{2,1,0:T(8,128)} %copy-done, f32[2,512]{1,0:T(2,128)S(1)} %dynamic-slice_bitcast_fusion.2, pred[512,4096]{1,0:T(8,128)(4,1)} %compare_and_fusion.5, bf16[512,2,32]{0,2,1:T(8,128)(2,1)} %bitcast.191, ...), kind=kOutput, calls=%fused_computation.13.clone.1 | convolution fusion | flops 289405952 | bytes 36249600 | tf_op jit(solution)/shard_map/while/body/eval_jaxpr/qhd,khd->hqk/dot_general | solution.py:117
  712.1 12.5 multiply_convert_fusion.4
  748.4 7.9 fusion.152
  756.3 15.4 %multiply_reduce_fusion.7 = (f32[2,512]{1,0:T(2,128)S(1)}, f32[2,512,4096]{2,1,0:T(8,128)}) fusion(f32[2,512,4096]{2,1,0:T(8,128)} %copy-done, f32[2,512]{1,0:T(2,128)S(1)} %dynamic-slice_bitcast_fusion.2, pred[512,4096]{1,0:T(8,128)(4,1)} %compare_and_fusion.5, bf16[512,2,32]{0,2,1:T(8,128)(2,1)} %bitcast.191, ...), kind=kOutput, calls=%fused_computation.13.clone.1 | convolution fusion | flops 289405952 | bytes 36249600 | tf_op jit(solution)/shard_map/while/body/eval_jaxpr/qhd,khd->hqk/dot_general | solution.py:117
  771.7 12.4 multiply_convert_fusion.4
  808.0 7.9 fusion.152
  815.9 15.4 %multiply_reduce_fusion.7 = (f32[2,512]{1,0:T(2,128)S(1)}, f32[2,512,4096]{2,1,0:T(8,128)}) fusion(f32[2,512,4096]{2,1,0:T(8,128)} %copy-done, f32[2,512]{1,0:T(2,128)S(1)} %dynamic-slice_bitcast_fusion.2, pred[512,4096]{1,0:T(8,128)(4,1)} %compare_and_fusion.5, bf16[512,2,32]{0,2,1:T(8,128)(2,1)} %bitcast.191, ...), kind=kOutput, calls=%fused_computation.13.clone.1 | convolution fusion | flops 289405952 | bytes 36249600 | tf_op jit(solution)/shard_map/while/body/eval_jaxpr/qhd,khd->hqk/dot_general | solution.py:117
  831.3 12.4 multiply_convert_fusion.4
  867.6 7.9 fusion.152
  875.5 15.4 %multiply_reduce_fusion.7 = (f32[2,512]{1,0:T(2,128)S(1)}, f32[2,512,4096]{2,1,0:T(8,128)}) fusion(f32[2,512,4096]{2,1,0:T(8,128)} %copy-done, f32[2,512]{1,0:T(2,128)S(1)} %dynamic-slice_bitcast_fusion.2, pred[512,4096]{1,0:T(8,128)(4,1)} %compare_and_fusion.5, bf16[512,2,32]{0,2,1:T(8,128)(2,1)} %bitcast.191, ...), kind=kOutput, calls=%fused_computation.13.clone.1 | convolution fusion | flops 289405952 | bytes 36249600 | tf_op jit(solution)/shard_map/while/body/eval_jaxpr/qhd,khd->hqk/dot_general | solution.py:117
  890.9 12.4 multiply_convert_fusion.4
  921.4 5.7 copy-done
  927.1 7.9 fusion.152
  935.1 15.4 %multiply_reduce_fusion.7 = (f32[2,512]{1,0:T(2,128)S(1)}, f32[2,512,4096]{2,1,0:T(8,128)}) fusion(f32[2,512,4096]{2,1,0:T(8,128)} %copy-done, f32[2,512]{1,0:T(2,128)S(1)} %dynamic-slice_bitcast_fusion.2, pred[512,4096]{1,0:T(8,128)(4,1)} %compare_and_fusion.5, bf16[512,2,32]{0,2,1:T(8,128)(2,1)} %bitcast.191, ...), kind=kOutput, calls=%fused_computation.13.clone.1 | convolution fusion | flops 289405952 | bytes 36249600 | tf_op jit(solution)/shard_map/while/body/eval_jaxpr/qhd,khd->hqk/dot_general | solution.py:117
  950.5 12.4 multiply_convert_fusion.4
  981.0 5.7 copy-done
  986.7 7.9 fusion.152
  994.7 15.4 %multiply_reduce_fusion.7 = (f32[2,512]{1,0:T(2,128)S(1)}, f32[2,512,4096]{2,1,0:T(8,128)}) fusion(f32[2,512,4096]{2,1,0:T(8,128)} %copy-done, f32[2,512]{1,0:T(2,128)S(1)} %dynamic-slice_bitcast_fusion.2, pred[512,4096]{1,0:T(8,128)(4,1)} %compare_and_fusion.5, bf16[512,2,32]{0,2,1:T(8,128)(2,1)} %bitcast.191, ...), kind=kOutput, calls=%fused_computation.13.clone.1 | convolution fusion | flops 289405952 | bytes 36249600 | tf_op jit(solution)/shard_map/while/body/eval_jaxpr/qhd,khd->hqk/dot_general | solution.py:117
  1010.1 12.4 multiply_convert_fusion.4
  1040.6 5.7 copy-done
  1046.3 7.9 fusion.152
  1054.2 15.4 %multiply_reduce_fusion.7 = (f32[2,512]{1,0:T(2,128)S(1)}, f32[2,512,4096]{2,1,0:T(8,128)}) fusion(f32[2,512,4096]{2,1,0:T(8,128)} %copy-done, f32[2,512]{1,0:T(2,128)S(1)} %dynamic-slice_bitcast_fusion.2, pred[512,4096]{1,0:T(8,128)(4,1)} %compare_and_fusion.5, bf16[512,2,32]{0,2,1:T(8,128)(2,1)} %bitcast.191, ...), kind=kOutput, calls=%fused_computation.13.clone.1 | convolution fusion | flops 289405952 | bytes 36249600 | tf_op jit(solution)/shard_map/while/body/eval_jaxpr/qhd,khd->hqk/dot_general | solution.py:117
  1069.6 12.4 multiply_convert_fusion.4
  1119.9 21.4 %all-reduce.4 = (f32[2,64]{1,0:T(2,128)S(1)}, f32[512]{0:T(512)S(1)}) all-reduce(f32[2,64]{1,0:T(2,128)S(1)} %pad_maximum_fusion.1, f32[512]{0:T(512)S(1)} %copy-done.57), channel_id=7, replica_groups=mesh['dp'=8,'tensor'=4] {'dp'}, use_global_device_ids=true, to_apply=%region_32.33.clone | all-reduce | flops 640 | bytes 5120
  1142.6 23.4 %reduce-scatter.14.cloned.1.call-done = f32[32,6]{1,0:T(8,128)} async-done(((f32[256,6]{1,0:T(8,128)}), f32[32,6]{1,0:T(8,128)}) %reduce-scatter.14.cloned.1.call-update) | async-done | bytes 784
  1167.4 62.7 %reduce-scatter.8.cloned.1.call-done = f32[64,32]{0,1:T(8,128)} async-done(((f32[64,256]{0,1:T(8,128)}), f32[64,32]{0,1:T(8,128)}) %reduce-scatter.8.cloned.1.call-update) | async-done | bytes 8208 | tf_op jit(solution)/shard_map/reduce_scatter | solution.py:269
  1231.5 73.8 %all-reduce.19.cloned.1.call-done = f32[3,256,64]{2,0,1:T(4,128)} async-done(((f32[3,256,64]{2,0,1:T(4,128)}), f32[3,256,64]{2,0,1:T(4,128)}) %all-reduce.19.cloned.1.call-update) | async-done | bytes 196624
  1306.9 85.6 %all-reduce.17.cloned.1.call-done = f32[4096,256]{1,0:T(8,128)} async-done(((f32[4096,256]{1,0:T(8,128)}), f32[4096,256]{1,0:T(8,128)}) %all-reduce.17.cloned.1.call-update) | async-done | bytes 4194320 | tf_op jit(solution)/shard_map/psum | solution.py:56
  1392.5 6.0 add.296
  (457 shorter events, 393.8 us)
Async XLA Ops:
  7.2 91.4 %copy-start.12 = (bf16[4096,256]{1,0:T(8,128)(2,1)S(1)}, bf16[4096,256]{1,0:T(8,128)(2,1)}, u32[]{:S(2)}) copy-start(bf16[4096,256]{1,0:T(8,128)(2,1)} %param.30) | copy-start | bytes 6291460
  7.2 357.7 %all-reduce.11.cloned.1.call-start = ((), (), s32[]{:S(2)}) async-start(), calls=%async_computation.4 | async-start | bytes 8388608 | tf_op jit(solution)/shard_map/psum | solution.py:56
  101.7 153.8 %copy-start.29 = (bf16[64,256]{0,1:T(8,128)(2,1)S(1)}, bf16[64,256]{0,1:T(8,128)(2,1)}, u32[]{:S(2)}) copy-start(bf16[64,256]{0,1:T(8,128)(2,1)} %all_gather.23) | copy-start | bytes 98308
  255.5 21.8 %copy-start.46 = (f32[6,32]{1,0:T(8,128)S(1)}, f32[6,32]{1,0:T(8,128)}, u32[]{:S(2)}) copy-start(f32[6,32]{1,0:T(8,128)} %param.39) | copy-start | bytes 2308
  255.5 47.9 %copy-start.33 = (f32[32,512]{1,0:T(8,128)S(1)}, f32[32,512]{1,0:T(8,128)}, u32[]{:S(2)}) copy-start(f32[32,512]{1,0:T(8,128)} %param.37) | copy-start | bytes 196612
  255.5 47.9 %copy-start.31 = (f32[512,32]{0,1:T(8,128)S(1)}, f32[512,32]{0,1:T(8,128)}, u32[]{:S(2)}) copy-start(f32[512,32]{0,1:T(8,128)} %param.38) | copy-start | bytes 196612
  255.5 109.5 %copy-start.13 = (bf16[4096,256]{1,0:T(8,128)(2,1)S(1)}, bf16[4096,256]{1,0:T(8,128)(2,1)}, u32[]{:S(2)}) copy-start(bf16[4096,256]{1,0:T(8,128)(2,1)} %param.30) | copy-start | bytes 6291460
  258.3 223.1 %all-reduce.13.cloned.1.call-start = ((), (), s32[]{:S(2)}) async-start(), calls=%async_computation.5 | async-start | bytes 8388608 | tf_op jit(solution)/shard_map/psum | solution.py:56
  371.5 21.6 %copy-start.24 = (bf16[4096,256]{1,0:T(8,128)(2,1)}, bf16[4096,256]{1,0:T(8,128)(2,1)S(1)}, u32[]{:S(2)}) copy-start(bf16[4096,256]{1,0:T(8,128)(2,1)S(1)} %fusion.36) | copy-start | bytes 6291460
  398.5 197.3 %all-reduce.15.cloned.1.call-start = ((), (), s32[]{:S(2)}) async-start(), calls=%async_computation.6 | async-start | bytes 8388608 | tf_op jit(solution)/shard_map/psum | solution.py:56
  510.0 606.4 %reduce-scatter.12.cloned.1.call-start = ((), (), s32[]{:S(2)}) async-start(), calls=%async_computation.10 | async-start | bytes 589824 | tf_op jit(solution)/shard_map/reduce_scatter | solution.py:271
  515.7 602.4 %reduce-scatter.10.cloned.1.call-start = ((), (), s32[]{:S(2)}) async-start(), calls=%async_computation.9 | async-start | bytes 589824 | tf_op jit(solution)/shard_map/reduce_scatter | solution.py:270
  520.9 645.1 %reduce-scatter.14.cloned.1.call-start = ((), (), s32[]{:S(2)}) async-start(), calls=%async_computation.11 | async-start | bytes 147456
  637.0 15.4 %copy-start.1 = (pred[512,4096]{1,0:T(8,128)(4,1)S(1)}, pred[512,4096]{1,0:T(8,128)(4,1)}, u32[]{:S(2)}) copy-start(pred[512,4096]{1,0:T(8,128)(4,1)} %compare_and_fusion.5) | copy-start | bytes 6291460 | tf_op jit(solution)/shard_map/while
  652.4 12.5 copy-start.6
  696.7 15.4 %copy-start.1 = (pred[512,4096]{1,0:T(8,128)(4,1)S(1)}, pred[512,4096]{1,0:T(8,128)(4,1)}, u32[]{:S(2)}) copy-start(pred[512,4096]{1,0:T(8,128)(4,1)} %compare_and_fusion.5) | copy-start | bytes 6291460 | tf_op jit(solution)/shard_map/while
  712.1 12.5 copy-start.6
  756.3 15.4 %copy-start.1 = (pred[512,4096]{1,0:T(8,128)(4,1)S(1)}, pred[512,4096]{1,0:T(8,128)(4,1)}, u32[]{:S(2)}) copy-start(pred[512,4096]{1,0:T(8,128)(4,1)} %compare_and_fusion.5) | copy-start | bytes 6291460 | tf_op jit(solution)/shard_map/while
  771.7 12.4 copy-start.6
  815.9 15.4 %copy-start.1 = (pred[512,4096]{1,0:T(8,128)(4,1)S(1)}, pred[512,4096]{1,0:T(8,128)(4,1)}, u32[]{:S(2)}) copy-start(pred[512,4096]{1,0:T(8,128)(4,1)} %compare_and_fusion.5) | copy-start | bytes 6291460 | tf_op jit(solution)/shard_map/while
  831.3 12.4 copy-start.6
  875.5 15.4 %copy-start.1 = (pred[512,4096]{1,0:T(8,128)(4,1)S(1)}, pred[512,4096]{1,0:T(8,128)(4,1)}, u32[]{:S(2)}) copy-start(pred[512,4096]{1,0:T(8,128)(4,1)} %compare_and_fusion.5) | copy-start | bytes 6291460 | tf_op jit(solution)/shard_map/while
  890.9 12.4 copy-start.6
  935.1 15.4 %copy-start.1 = (pred[512,4096]{1,0:T(8,128)(4,1)S(1)}, pred[512,4096]{1,0:T(8,128)(4,1)}, u32[]{:S(2)}) copy-start(pred[512,4096]{1,0:T(8,128)(4,1)} %compare_and_fusion.5) | copy-start | bytes 6291460 | tf_op jit(solution)/shard_map/while
  950.5 12.4 copy-start.6
  994.7 15.4 %copy-start.1 = (pred[512,4096]{1,0:T(8,128)(4,1)S(1)}, pred[512,4096]{1,0:T(8,128)(4,1)}, u32[]{:S(2)}) copy-start(pred[512,4096]{1,0:T(8,128)(4,1)} %compare_and_fusion.5) | copy-start | bytes 6291460 | tf_op jit(solution)/shard_map/while
  1010.1 12.4 copy-start.6
  1054.2 15.4 %copy-start.1 = (pred[512,4096]{1,0:T(8,128)(4,1)S(1)}, pred[512,4096]{1,0:T(8,128)(4,1)}, u32[]{:S(2)}) copy-start(pred[512,4096]{1,0:T(8,128)(4,1)} %compare_and_fusion.5) | copy-start | bytes 6291460 | tf_op jit(solution)/shard_map/while
  1069.6 12.4 copy-start.6
  1104.9 125.2 %reduce-scatter.8.cloned.1.call-start = ((), (), s32[]{:S(2)}) async-start(), calls=%async_computation.8 | async-start | bytes 147456 | tf_op jit(solution)/shard_map/reduce_scatter | solution.py:269
  1105.7 199.7 %all-reduce.19.cloned.1.call-start = ((), (), s32[]{:S(2)}) async-start(), calls=%async_computation.12 | async-start | bytes 1048576
  1109.0 283.5 %all-reduce.17.cloned.1.call-start = ((), (), s32[]{:S(2)}) async-start(), calls=%async_computation.7 | async-start | bytes 8388608 | tf_op jit(solution)/shard_map/psum | solution.py:56
  1114.1 27.2 %copy-start.62 = (f32[64]{0:T(128)S(1)}, f32[64]{0:T(128)}, u32[]{:S(2)}) copy-start(f32[64]{0:T(128)} %param.41) | copy-start | bytes 772
  1114.1 27.2 %copy-start.63 = (f32[64]{0:T(128)S(1)}, f32[64]{0:T(128)}, u32[]{:S(2)}) copy-start(f32[64]{0:T(128)} %param.48) | copy-start | bytes 772
  1114.1 27.2 %copy-start.64 = (f32[64]{0:T(128)S(1)}, f32[64]{0:T(128)}, u32[]{:S(2)}) copy-start(f32[64]{0:T(128)} %param.55) | copy-start | bytes 772
  1114.1 27.8 %copy-start.58 = (f32[2,8]{1,0:T(2,128)S(1)}, f32[2,8]{1,0:T(2,128)}, u32[]{:S(2)}) copy-start(f32[2,8]{1,0:T(2,128)} %param.40) | copy-start | bytes 196
  1114.1 27.8 %copy-start.59 = (f32[2,8]{1,0:T(2,128)S(1)}, f32[2,8]{1,0:T(2,128)}, u32[]{:S(2)}) copy-start(f32[2,8]{1,0:T(2,128)} %param.47) | copy-start | bytes 196
  1114.1 27.7 %copy-start.60 = (f32[2,8]{1,0:T(2,128)S(1)}, f32[2,8]{1,0:T(2,128)}, u32[]{:S(2)}) copy-start(f32[2,8]{1,0:T(2,128)} %param.54) | copy-start | bytes 196
  1114.1 52.6 %copy-start.47 = (f32[6,32]{1,0:T(8,128)S(1)}, f32[6,32]{1,0:T(8,128)}, u32[]{:S(2)}) copy-start(f32[6,32]{1,0:T(8,128)} %param.39) | copy-start | bytes 2308
  1114.2 52.6 %copy-start.53 = (f32[6,32]{1,0:T(8,128)S(1)}, f32[6,32]{1,0:T(8,128)}, u32[]{:S(2)}) copy-start(f32[6,32]{1,0:T(8,128)} %param.46) | copy-start | bytes 2308
  1114.2 52.6 %copy-start.54 = (f32[6,32]{1,0:T(8,128)S(1)}, f32[6,32]{1,0:T(8,128)}, u32[]{:S(2)}) copy-start(f32[6,32]{1,0:T(8,128)} %param.53) | copy-start | bytes 2308
  1114.2 116.0 %copy-start.40 = (f32[64,32]{0,1:T(8,128)S(1)}, f32[64,32]{0,1:T(8,128)}, u32[]{:S(2)}) copy-start(f32[64,32]{0,1:T(8,128)} %param.36) | copy-start | bytes 24580
  1114.2 116.0 %copy-start.43 = (f32[64,32]{0,1:T(8,128)S(1)}, f32[64,32]{0,1:T(8,128)}, u32[]{:S(2)}) copy-start(f32[64,32]{0,1:T(8,128)} %param.43) | copy-start | bytes 24580
  1114.2 115.9 %copy-start.44 = (f32[64,32]{0,1:T(8,128)S(1)}, f32[64,32]{0,1:T(8,128)}, u32[]{:S(2)}) copy-start(f32[64,32]{0,1:T(8,128)} %param.50) | copy-start | bytes 24580
  1114.2 192.0 %copy-start.35 = (f32[3,32,64]{2,1,0:T(8,128)S(1)}, f32[3,32,64]{2,1,0:T(8,128)}, u32[]{:S(2)}) copy-start(f32[3,32,64]{2,1,0:T(8,128)} %param.35) | copy-start | bytes 73732
  1114.2 192.0 %copy-start.41 = (f32[3,32,64]{2,1,0:T(8,128)S(1)}, f32[3,32,64]{2,1,0:T(8,128)}, u32[]{:S(2)}) copy-start(f32[3,32,64]{2,1,0:T(8,128)} %param.42) | copy-start | bytes 73732
  1114.2 192.0 %copy-start.42 = (f32[3,32,64]{2,1,0:T(8,128)S(1)}, f32[3,32,64]{2,1,0:T(8,128)}, u32[]{:S(2)}) copy-start(f32[3,32,64]{2,1,0:T(8,128)} %param.49) | copy-start | bytes 73732
  1166.8 231.7 %copy-start.45 = (f32[6,32]{1,0:T(8,128)}, f32[6,32]{1,0:T(8,128)S(1)}, u32[]{:S(2)}) copy-start(f32[6,32]{1,0:T(8,128)S(1)} %copy.106) | copy-start | bytes 2308
  (70 other events, 323.6 us)
Sparse Core Ops, SparseCore 0:
  258.4 82.8 all-reduce.10
  398.6 82.7 all-reduce.12
  510.1 85.6 all-reduce.14
  599.9 61.9 reduce-scatter.11
  665.7 60.9 reduce-scatter.9
  1105.0 60.9 reduce-scatter.13
  1170.2 59.8 reduce-scatter.7
  1233.9 71.3 all-reduce.18
  1307.7 84.7 all-reduce.16
where the time goes:
time: 1420 us; the launch traced here: 1410 us
  waiting for transfers between devices  404 us (28%)
  matrix products  392 us (28%)
  other arithmetic  240 us (17%)
  blocking collectives  211 us (15%)
  local copies, waits for them, and re-layouts  113 us (8%)
  loops' own time  27.3 us (2%)
  between operations  17.7 us (1%)
    psum x4, waiting for transfers between devices, summed(): return lax.psum(partial_value, 'tensor')  243 us
    dot_general x8, matrix products, one_block(): jnp.einsum('qhd,khd->hqk', grad_block, value_heads, preferred_element_typ...  123 us
    convert_element_type x8, other arithmetic, one_block(): score_grad = (probs * (prob_grad - delta)).astype(jnp.bfloat16)  99.3 us
    unnamed x11, waiting for transfers between devices  97.6 us
    dot_general x8, matrix products, one_block(): jnp.einsum('hqk,qhd->khd', probs.astype(jnp.bfloat16), grad_block, prefer...  63.3 us
    reduce_scatter x1, waiting for transfers between devices, body(): lax.psum_scatter(grad_outward, 'dp', scatter_dimension=1, tiled=True)  62.7 us
    dot_general x16, matrix products, mask_scores(): jnp.einsum('qhd,khd->hqk', query_block, key_heads, preferred_element_type...  58.8 us
    and x16, other arithmetic, mask_scores(): allowed = (seg_block[:, None] == segment[None, :]) & key_open[None, :]  46.6 us
  transfers between devices with their start and end apart: 9, of which 6 were waited for; matrix products, arithmetic and copies ran while one was open for 33% of the time, Pallas kernels for 0%

commit v1 on v0

--- a/solution.py
+++ b/solution.py
@@ -53,7 +53,7 @@
 
 
 def summed(partial_value):
-    return lax.psum(partial_value, "tensor")
+    return jnp.sum(lax.all_gather(partial_value, "tensor"), 0)
 
 
 def mask_scores(query_block, key_heads, seg_block, segment, key_open):

time: 1420 us -> 1510 us (1.063)
  waiting for transfers between devices: 404 us -> 462 us
  other arithmetic: 240 us -> 277 us
    all_gather x0 -> x4, waiting for transfers between devices: none -> 303 us  [summed(): return jnp.sum(lax.all_gather(partial_value, 'tensor'), 0)]
    psum x4 -> x0, waiting for transfers between devices: 243 us -> none  [summed(): return lax.psum(partial_value, 'tensor')]
    reduce_sum x0 -> x4, other arithmetic: none -> 37.8 us  [summed(): return jnp.sum(lax.all_gather(partial_value, 'tensor'), 0)]
  transfers between devices with their start and end apart: 9 -> 9, of which waited for: 6 -> 6; matrix products, arithmetic and copies ran while one was open for 33% -> 32% of each run, Pallas kernels for 0% -> 0%
where the time goes in v1:
time: 1510 us; the launch traced here: 1500 us
  waiting for transfers between devices  462 us (31%)
  matrix products  393 us (26%)
  other arithmetic  277 us (18%)
  blocking collectives  212 us (14%)
  local copies, waits for them, and re-layouts  111 us (7%)
  loops' own time  27.1 us (2%)
  between operations  17.9 us (1%)
    all_gather x4, waiting for transfers between devices, summed(): return jnp.sum(lax.all_gather(partial_value, 'tensor'), 0)  303 us
    dot_general x8, matrix products, one_block(): jnp.einsum('qhd,khd->hqk', grad_block, value_heads, preferred_element_typ...  124 us
    convert_element_type x8, other arithmetic, one_block(): score_grad = (probs * (prob_grad - delta)).astype(jnp.bfloat16)  99.2 us
    unnamed x11, waiting for transfers between devices  97.3 us
    dot_general x8, matrix products, one_block(): jnp.einsum('hqk,qhd->khd', probs.astype(jnp.bfloat16), grad_block, prefer...  63.3 us
    reduce_scatter x1, waiting for transfers between devices, body(): lax.psum_scatter(grad_outward, 'dp', scatter_dimension=1, tiled=True)  62.4 us
    dot_general x16, matrix products, mask_scores(): jnp.einsum('qhd,khd->hqk', query_block, key_heads, preferred_element_type...  58.8 us
    while x96, local copies, waits for them, and re-layouts  46 us
  transfers between devices with their start and end apart: 9, of which 6 were waited for; matrix products, arithmetic and copies ran while one was open for 32% of the time, Pallas kernels for 0%

profile of v1, /device:TPU:0, one launch (start us, length us, event | category | flops | bytes accessed | tf_op | source)
XLA Modules:
  0.0 1501.0 jit_solution(12841025670019200616)
XLA Ops:
  8.1 22.1 %all-gather.4 = bf16[8,8,2]{1,2,0:T(2,128)(2,1)S(1)} all-gather(bf16[1,8,2]{1,2,0:T(2,128)(2,1)S(1)} %convert_bitcast_fusion.2), channel_id=1, replica_groups=mesh['dp'=8,'tensor'=4] {'dp'}, dimensions={0}, use_global_device_ids=true | all-gather | bytes 288 | tf_op jit(solution)/shard_map/all_gather | solution.py:195
  32.6 32.5 %all_gather.47 = bf16[64,256]{0,1:T(8,128)(2,1)} all-gather(bf16[64,32]{0,1:T(8,128)(2,1)S(1)} %convert_element_type.133), channel_id=1, replica_groups=mesh['dp'=8,'tensor'=4] {'dp'}, dimensions={1}, use_global_device_ids=true | all-gather | bytes 36864 | tf_op jit(solution)/shard_map/all_gather | solution.py:191
  65.1 30.6 %all_gather.45 = bf16[3,256,64]{2,1,0:T(8,128)(2,1)S(1)} all-gather(bf16[3,32,64]{2,1,0:T(8,128)(2,1)S(1)} %convert_element_type.125), channel_id=1, replica_groups=mesh['dp'=8,'tensor'=4] {'dp'}, dimensions={1}, use_global_device_ids=true | all-gather | bytes 110592 | tf_op jit(solution)/shard_map/all_gather | solution.py:190
  101.7 152.2 %while.27 = (s32[]{:T(128)}, bf16[8,512,64]{1,2,0:T(8,128)(2,1)S(1)}, f32[8,2,512]{2,1,0:T(2,128)}, s32[8]{0:T(128)S(1)}, s32[4096]{0:T(1024)}, /*index=5*/s32[1...) while((s32[]{:T(128)}, ...), condition=%wide.region_3.4_spmd, body=%wide.region_0.3_spmd.sunk | while | flops 591395840 | bytes 60221656 | solution.py:93
  258.4 17.4 %all-reduce = bf16[512]{0:T(512)(128)(2,1)S(1)} all-reduce(bf16[512]{0:T(512)(128)(2,1)S(1)} %dynamic-update-slice), channel_id=1, replica_groups=mesh['dp'=8,'tensor'=4] {'dp'}, use_global_device_ids=true, to_apply=%add | all-reduce | flops 512 | bytes 2048
  275.8 26.0 %all-gather.5 = bf16[8,32,6]{1,2,0:T(8,128)(2,1)S(1)} all-gather(bf16[1,32,6]{1,2,0:T(8,128)(2,1)S(1)} %convert_bitcast_fusion.1), channel_id=1, replica_groups=mesh['dp'=8,'tensor'=4] {'dp'}, dimensions={0}, use_global_device_ids=true | all-gather | bytes 3456 | tf_op jit(solution)/shard_map/all_gather | solution.py:194
  302.0 30.9 %all_gather.53 = bf16[512,256]{0,1:T(8,128)(2,1)S(1)} all-gather(bf16[512,32]{0,1:T(8,128)(2,1)S(1)} %convert_element_type.141), channel_id=1, replica_groups=mesh['dp'=8,'tensor'=4] {'dp'}, dimensions={1}, use_global_device_ids=true | all-gather | bytes 294912 | tf_op jit(solution)/shard_map/all_gather | solution.py:193
  332.9 30.7 %all_gather.51 = bf16[256,512]{1,0:T(8,128)(2,1)S(1)} all-gather(bf16[32,512]{1,0:T(8,128)(2,1)S(1)} %convert_element_type.137), channel_id=1, replica_groups=mesh['dp'=8,'tensor'=4] {'dp'}, dimensions={0}, use_global_device_ids=true | all-gather | bytes 294912 | tf_op jit(solution)/shard_map/all_gather | solution.py:192
  363.6 9.6 reduce_sum.207
  379.7 21.6 %multiply_convert_fusion.1 = (bf16[4096,512]{1,0:T(8,128)(2,1)S(1)}, f32[4096,512]{1,0:T(8,128)}, f32[4096,512]{1,0:T(8,128)}) fusion(f32[512]{0:T(512)S(1)} %convert_element_type.139, bf16[4096,256]{1,0:T(8,128)(2,1)S(1)} %fusion.36, bf16[256,512]{1,0:T(8,128)(2,1)S(1)} %all_gather.51), kind=kOutput, calls=%fused_computation.35 | convolution fusion | flops 1212153856 | bytes 23332864 | tf_op jit(solution)/shard_map/dot_general | solution.py:19
  407.2 102.9 %all-gather.13.cloned.1.call-done = f32[16384,256]{1,0:T(8,128)} async-done(((f32[4096,256]{1,0:T(8,128)}), f32[16384,256]{1,0:T(8,128)}) %all-gather.13.cloned.1.call-update) | async-done | bytes 16777232 | tf_op jit(solution)/shard_map/all_gather | solution.py:56
  510.0 9.5 reduce_sum.210
  534.2 8.6 convert_reduce_fusion
  559.7 94.5 %all-gather.15.cloned.1.call-done = f32[16384,256]{1,0:T(8,128)} async-done(((f32[4096,256]{1,0:T(8,128)}), f32[16384,256]{1,0:T(8,128)}) %all-gather.15.cloned.1.call-update) | async-done | bytes 16777232 | tf_op jit(solution)/shard_map/all_gather | solution.py:56
  654.2 9.4 reduce_sum.215
  663.6 6.8 multiply_reduce_fusion.1
  677.7 476.8 %while.28 = (s32[]{:T(128)}, f32[4096,2,32]{0,2,1:T(8,128)S(1)}, f32[4096,2,32]{0,2,1:T(8,128)}, bf16[8,512,64]{1,2,0:T(8,128)(2,1)}, s32[8]{0:T(128)S(1)}, /*in...) while((s32[]{:T(128)}, f32[4096,2,32]{0,2,1:T(8,128)S(1)}, ...), condition=%wide.region_17.18_spmd.clone, body=%wide.region_15.17_spmd.clone.sunk | while | flops 1410399232 | bytes 220977600 | solution.py:141
  696.8 7.7 fusion.152
  704.5 15.5 %multiply_reduce_fusion.7 = (f32[2,512]{1,0:T(2,128)S(1)}, f32[2,512,4096]{2,1,0:T(8,128)}) fusion(f32[2,512,4096]{2,1,0:T(8,128)} %copy-done, f32[2,512]{1,0:T(2,128)S(1)} %dynamic-slice_bitcast_fusion.2, pred[512,4096]{1,0:T(8,128)(4,1)} %compare_and_fusion.5, bf16[512,2,32]{0,2,1:T(8,128)(2,1)} %bitcast.199, ...), kind=kOutput, calls=%fused_computation.13.clone.1 | convolution fusion | flops 289405952 | bytes 36249600 | tf_op jit(solution)/shard_map/while/body/eval_jaxpr/qhd,khd->hqk/dot_general | solution.py:117
  719.9 12.4 multiply_convert_fusion.4
  756.1 8.0 fusion.152
  764.1 15.5 %multiply_reduce_fusion.7 = (f32[2,512]{1,0:T(2,128)S(1)}, f32[2,512,4096]{2,1,0:T(8,128)}) fusion(f32[2,512,4096]{2,1,0:T(8,128)} %copy-done, f32[2,512]{1,0:T(2,128)S(1)} %dynamic-slice_bitcast_fusion.2, pred[512,4096]{1,0:T(8,128)(4,1)} %compare_and_fusion.5, bf16[512,2,32]{0,2,1:T(8,128)(2,1)} %bitcast.199, ...), kind=kOutput, calls=%fused_computation.13.clone.1 | convolution fusion | flops 289405952 | bytes 36249600 | tf_op jit(solution)/shard_map/while/body/eval_jaxpr/qhd,khd->hqk/dot_general | solution.py:117
  779.6 12.5 multiply_convert_fusion.4
  815.8 7.9 fusion.152
  823.7 15.5 %multiply_reduce_fusion.7 = (f32[2,512]{1,0:T(2,128)S(1)}, f32[2,512,4096]{2,1,0:T(8,128)}) fusion(f32[2,512,4096]{2,1,0:T(8,128)} %copy-done, f32[2,512]{1,0:T(2,128)S(1)} %dynamic-slice_bitcast_fusion.2, pred[512,4096]{1,0:T(8,128)(4,1)} %compare_and_fusion.5, bf16[512,2,32]{0,2,1:T(8,128)(2,1)} %bitcast.199, ...), kind=kOutput, calls=%fused_computation.13.clone.1 | convolution fusion | flops 289405952 | bytes 36249600 | tf_op jit(solution)/shard_map/while/body/eval_jaxpr/qhd,khd->hqk/dot_general | solution.py:117
  839.2 12.4 multiply_convert_fusion.4
  875.3 7.9 fusion.152
  883.3 15.5 %multiply_reduce_fusion.7 = (f32[2,512]{1,0:T(2,128)S(1)}, f32[2,512,4096]{2,1,0:T(8,128)}) fusion(f32[2,512,4096]{2,1,0:T(8,128)} %copy-done, f32[2,512]{1,0:T(2,128)S(1)} %dynamic-slice_bitcast_fusion.2, pred[512,4096]{1,0:T(8,128)(4,1)} %compare_and_fusion.5, bf16[512,2,32]{0,2,1:T(8,128)(2,1)} %bitcast.199, ...), kind=kOutput, calls=%fused_computation.13.clone.1 | convolution fusion | flops 289405952 | bytes 36249600 | tf_op jit(solution)/shard_map/while/body/eval_jaxpr/qhd,khd->hqk/dot_general | solution.py:117
  898.7 12.4 multiply_convert_fusion.4
  934.9 7.9 fusion.152
  942.9 15.5 %multiply_reduce_fusion.7 = (f32[2,512]{1,0:T(2,128)S(1)}, f32[2,512,4096]{2,1,0:T(8,128)}) fusion(f32[2,512,4096]{2,1,0:T(8,128)} %copy-done, f32[2,512]{1,0:T(2,128)S(1)} %dynamic-slice_bitcast_fusion.2, pred[512,4096]{1,0:T(8,128)(4,1)} %compare_and_fusion.5, bf16[512,2,32]{0,2,1:T(8,128)(2,1)} %bitcast.199, ...), kind=kOutput, calls=%fused_computation.13.clone.1 | convolution fusion | flops 289405952 | bytes 36249600 | tf_op jit(solution)/shard_map/while/body/eval_jaxpr/qhd,khd->hqk/dot_general | solution.py:117
  958.3 12.4 multiply_convert_fusion.4
  994.5 7.9 fusion.152
  1002.4 15.5 %multiply_reduce_fusion.7 = (f32[2,512]{1,0:T(2,128)S(1)}, f32[2,512,4096]{2,1,0:T(8,128)}) fusion(f32[2,512,4096]{2,1,0:T(8,128)} %copy-done, f32[2,512]{1,0:T(2,128)S(1)} %dynamic-slice_bitcast_fusion.2, pred[512,4096]{1,0:T(8,128)(4,1)} %compare_and_fusion.5, bf16[512,2,32]{0,2,1:T(8,128)(2,1)} %bitcast.199, ...), kind=kOutput, calls=%fused_computation.13.clone.1 | convolution fusion | flops 289405952 | bytes 36249600 | tf_op jit(solution)/shard_map/while/body/eval_jaxpr/qhd,khd->hqk/dot_general | solution.py:117
  1017.9 12.4 multiply_convert_fusion.4
  1054.0 7.9 fusion.152
  1062.0 15.5 %multiply_reduce_fusion.7 = (f32[2,512]{1,0:T(2,128)S(1)}, f32[2,512,4096]{2,1,0:T(8,128)}) fusion(f32[2,512,4096]{2,1,0:T(8,128)} %copy-done, f32[2,512]{1,0:T(2,128)S(1)} %dynamic-slice_bitcast_fusion.2, pred[512,4096]{1,0:T(8,128)(4,1)} %compare_and_fusion.5, bf16[512,2,32]{0,2,1:T(8,128)(2,1)} %bitcast.199, ...), kind=kOutput, calls=%fused_computation.13.clone.1 | convolution fusion | flops 289405952 | bytes 36249600 | tf_op jit(solution)/shard_map/while/body/eval_jaxpr/qhd,khd->hqk/dot_general | solution.py:117
  1077.5 12.4 multiply_convert_fusion.4
  1113.6 7.9 fusion.152
  1121.6 15.5 %multiply_reduce_fusion.7 = (f32[2,512]{1,0:T(2,128)S(1)}, f32[2,512,4096]{2,1,0:T(8,128)}) fusion(f32[2,512,4096]{2,1,0:T(8,128)} %copy-done, f32[2,512]{1,0:T(2,128)S(1)} %dynamic-slice_bitcast_fusion.2, pred[512,4096]{1,0:T(8,128)(4,1)} %compare_and_fusion.5, bf16[512,2,32]{0,2,1:T(8,128)(2,1)} %bitcast.199, ...), kind=kOutput, calls=%fused_computation.13.clone.1 | convolution fusion | flops 289405952 | bytes 36249600 | tf_op jit(solution)/shard_map/while/body/eval_jaxpr/qhd,khd->hqk/dot_general | solution.py:117
  1137.0 12.4 multiply_convert_fusion.4
  1187.0 21.3 %all-reduce.4 = (f32[2,64]{1,0:T(2,128)S(1)}, f32[512]{0:T(512)S(1)}) all-reduce(f32[2,64]{1,0:T(2,128)S(1)} %pad_maximum_fusion.1, f32[512]{0:T(512)S(1)} %copy-done.57), channel_id=11, replica_groups=mesh['dp'=8,'tensor'=4] {'dp'}, use_global_device_ids=true, to_apply=%region_32.33.clone | all-reduce | flops 640 | bytes 5120
  1209.7 23.4 %reduce-scatter.14.cloned.1.call-done = f32[32,6]{1,0:T(8,128)} async-done(((f32[256,6]{1,0:T(8,128)}), f32[32,6]{1,0:T(8,128)}) %reduce-scatter.14.cloned.1.call-update) | async-done | bytes 784
  1234.6 62.4 %reduce-scatter.8.cloned.1.call-done = f32[64,32]{0,1:T(8,128)} async-done(((f32[64,256]{0,1:T(8,128)}), f32[64,32]{0,1:T(8,128)}) %reduce-scatter.8.cloned.1.call-update) | async-done | bytes 8208 | tf_op jit(solution)/shard_map/reduce_scatter | solution.py:269
  1298.3 73.5 %all-reduce.7.cloned.1.call-done = f32[3,256,64]{2,0,1:T(4,128)} async-done(((f32[3,256,64]{2,0,1:T(4,128)}), f32[3,256,64]{2,0,1:T(4,128)}) %all-reduce.7.cloned.1.call-update) | async-done | bytes 196624
  1373.4 105.3 %all-gather.17.cloned.1.call-done = f32[16384,256]{1,0:T(8,128)} async-done(((f32[4096,256]{1,0:T(8,128)}), f32[16384,256]{1,0:T(8,128)}) %all-gather.17.cloned.1.call-update) | async-done | bytes 16777232 | tf_op jit(solution)/shard_map/all_gather | solution.py:56
  1478.7 9.4 reduce_sum.218
  1488.1 6.0 add.288
  (461 shorter events, 415.4 us)
Async XLA Ops:
  7.2 91.4 %copy-start.12 = (bf16[4096,256]{1,0:T(8,128)(2,1)S(1)}, bf16[4096,256]{1,0:T(8,128)(2,1)}, u32[]{:S(2)}) copy-start(bf16[4096,256]{1,0:T(8,128)(2,1)} %param.30) | copy-start | bytes 6291460
  7.2 356.4 %all-gather.11.cloned.1.call-start = ((), (), s32[]{:S(2)}) async-start(), calls=%async_computation.7 | async-start | bytes 20971520 | tf_op jit(solution)/shard_map/all_gather | solution.py:56
  101.7 152.3 %copy-start.29 = (bf16[64,256]{0,1:T(8,128)(2,1)S(1)}, bf16[64,256]{0,1:T(8,128)(2,1)}, u32[]{:S(2)}) copy-start(bf16[64,256]{0,1:T(8,128)(2,1)} %all_gather.47) | copy-start | bytes 98308
  254.0 21.9 %copy-start.46 = (f32[6,32]{1,0:T(8,128)S(1)}, f32[6,32]{1,0:T(8,128)}, u32[]{:S(2)}) copy-start(f32[6,32]{1,0:T(8,128)} %param.39) | copy-start | bytes 2308
  254.0 48.0 %copy-start.33 = (f32[32,512]{1,0:T(8,128)S(1)}, f32[32,512]{1,0:T(8,128)}, u32[]{:S(2)}) copy-start(f32[32,512]{1,0:T(8,128)} %param.37) | copy-start | bytes 196612
  254.0 48.0 %copy-start.31 = (f32[512,32]{0,1:T(8,128)S(1)}, f32[512,32]{0,1:T(8,128)}, u32[]{:S(2)}) copy-start(f32[512,32]{0,1:T(8,128)} %param.38) | copy-start | bytes 196612
  256.8 253.2 %all-gather.13.cloned.1.call-start = ((), (), s32[]{:S(2)}) async-start(), calls=%async_computation.8 | async-start | bytes 20971520 | tf_op jit(solution)/shard_map/all_gather | solution.py:56
  363.6 9.6 copy-start.13
  379.7 21.6 %copy-start.24 = (bf16[4096,256]{1,0:T(8,128)(2,1)}, bf16[4096,256]{1,0:T(8,128)(2,1)S(1)}, u32[]{:S(2)}) copy-start(bf16[4096,256]{1,0:T(8,128)(2,1)S(1)} %fusion.36) | copy-start | bytes 6291460
  406.7 247.5 %all-gather.15.cloned.1.call-start = ((), (), s32[]{:S(2)}) async-start(), calls=%async_computation.9 | async-start | bytes 20971520 | tf_op jit(solution)/shard_map/all_gather | solution.py:56
  548.1 635.6 %reduce-scatter.12.cloned.1.call-start = ((), (), s32[]{:S(2)}) async-start(), calls=%async_computation.6 | async-start | bytes 589824 | tf_op jit(solution)/shard_map/reduce_scatter | solution.py:271
  553.7 631.5 %reduce-scatter.10.cloned.1.call-start = ((), (), s32[]{:S(2)}) async-start(), calls=%async_computation.5 | async-start | bytes 589824 | tf_op jit(solution)/shard_map/reduce_scatter | solution.py:270
  559.7 673.5 %reduce-scatter.14.cloned.1.call-start = ((), (), s32[]{:S(2)}) async-start(), calls=%async_computation.11 | async-start | bytes 147456
  704.5 15.5 %copy-start.1 = (pred[512,4096]{1,0:T(8,128)(4,1)S(1)}, pred[512,4096]{1,0:T(8,128)(4,1)}, u32[]{:S(2)}) copy-start(pred[512,4096]{1,0:T(8,128)(4,1)} %compare_and_fusion.5) | copy-start | bytes 6291460 | tf_op jit(solution)/shard_map/while
  719.9 12.4 copy-start.6
  764.1 15.5 %copy-start.1 = (pred[512,4096]{1,0:T(8,128)(4,1)S(1)}, pred[512,4096]{1,0:T(8,128)(4,1)}, u32[]{:S(2)}) copy-start(pred[512,4096]{1,0:T(8,128)(4,1)} %compare_and_fusion.5) | copy-start | bytes 6291460 | tf_op jit(solution)/shard_map/while
  779.6 12.5 copy-start.6
  823.7 15.5 %copy-start.1 = (pred[512,4096]{1,0:T(8,128)(4,1)S(1)}, pred[512,4096]{1,0:T(8,128)(4,1)}, u32[]{:S(2)}) copy-start(pred[512,4096]{1,0:T(8,128)(4,1)} %compare_and_fusion.5) | copy-start | bytes 6291460 | tf_op jit(solution)/shard_map/while
  839.2 12.4 copy-start.6
  883.3 15.5 %copy-start.1 = (pred[512,4096]{1,0:T(8,128)(4,1)S(1)}, pred[512,4096]{1,0:T(8,128)(4,1)}, u32[]{:S(2)}) copy-start(pred[512,4096]{1,0:T(8,128)(4,1)} %compare_and_fusion.5) | copy-start | bytes 6291460 | tf_op jit(solution)/shard_map/while
  898.7 12.4 copy-start.6
  942.8 15.5 %copy-start.1 = (pred[512,4096]{1,0:T(8,128)(4,1)S(1)}, pred[512,4096]{1,0:T(8,128)(4,1)}, u32[]{:S(2)}) copy-start(pred[512,4096]{1,0:T(8,128)(4,1)} %compare_and_fusion.5) | copy-start | bytes 6291460 | tf_op jit(solution)/shard_map/while
  958.3 12.4 copy-start.6
  1002.4 15.5 %copy-start.1 = (pred[512,4096]{1,0:T(8,128)(4,1)S(1)}, pred[512,4096]{1,0:T(8,128)(4,1)}, u32[]{:S(2)}) copy-start(pred[512,4096]{1,0:T(8,128)(4,1)} %compare_and_fusion.5) | copy-start | bytes 6291460 | tf_op jit(solution)/shard_map/while
  1017.9 12.4 copy-start.6
  1062.0 15.5 %copy-start.1 = (pred[512,4096]{1,0:T(8,128)(4,1)S(1)}, pred[512,4096]{1,0:T(8,128)(4,1)}, u32[]{:S(2)}) copy-start(pred[512,4096]{1,0:T(8,128)(4,1)} %compare_and_fusion.5) | copy-start | bytes 6291460 | tf_op jit(solution)/shard_map/while
  1077.4 12.4 copy-start.6
  1121.6 15.5 %copy-start.1 = (pred[512,4096]{1,0:T(8,128)(4,1)S(1)}, pred[512,4096]{1,0:T(8,128)(4,1)}, u32[]{:S(2)}) copy-start(pred[512,4096]{1,0:T(8,128)(4,1)} %compare_and_fusion.5) | copy-start | bytes 6291460 | tf_op jit(solution)/shard_map/while
  1137.0 12.4 copy-start.6
  1172.2 124.8 %reduce-scatter.8.cloned.1.call-start = ((), (), s32[]{:S(2)}) async-start(), calls=%async_computation.4 | async-start | bytes 147456 | tf_op jit(solution)/shard_map/reduce_scatter | solution.py:269
  1172.9 198.9 %all-reduce.7.cloned.1.call-start = ((), (), s32[]{:S(2)}) async-start(), calls=%async_computation.12 | async-start | bytes 1048576
  1176.3 302.4 %all-gather.17.cloned.1.call-start = ((), (), s32[]{:S(2)}) async-start(), calls=%async_computation.10 | async-start | bytes 20971520 | tf_op jit(solution)/shard_map/all_gather | solution.py:56
  1181.2 27.1 %copy-start.62 = (f32[64]{0:T(128)S(1)}, f32[64]{0:T(128)}, u32[]{:S(2)}) copy-start(f32[64]{0:T(128)} %param.41) | copy-start | bytes 772
  1181.3 27.1 %copy-start.63 = (f32[64]{0:T(128)S(1)}, f32[64]{0:T(128)}, u32[]{:S(2)}) copy-start(f32[64]{0:T(128)} %param.48) | copy-start | bytes 772
  1181.3 27.1 %copy-start.64 = (f32[64]{0:T(128)S(1)}, f32[64]{0:T(128)}, u32[]{:S(2)}) copy-start(f32[64]{0:T(128)} %param.55) | copy-start | bytes 772
  1181.3 27.7 %copy-start.58 = (f32[2,8]{1,0:T(2,128)S(1)}, f32[2,8]{1,0:T(2,128)}, u32[]{:S(2)}) copy-start(f32[2,8]{1,0:T(2,128)} %param.40) | copy-start | bytes 196
  1181.3 27.7 %copy-start.59 = (f32[2,8]{1,0:T(2,128)S(1)}, f32[2,8]{1,0:T(2,128)}, u32[]{:S(2)}) copy-start(f32[2,8]{1,0:T(2,128)} %param.47) | copy-start | bytes 196
  1181.3 27.7 %copy-start.60 = (f32[2,8]{1,0:T(2,128)S(1)}, f32[2,8]{1,0:T(2,128)}, u32[]{:S(2)}) copy-start(f32[2,8]{1,0:T(2,128)} %param.54) | copy-start | bytes 196
  1181.3 52.6 %copy-start.47 = (f32[6,32]{1,0:T(8,128)S(1)}, f32[6,32]{1,0:T(8,128)}, u32[]{:S(2)}) copy-start(f32[6,32]{1,0:T(8,128)} %param.39) | copy-start | bytes 2308
  1181.3 52.6 %copy-start.53 = (f32[6,32]{1,0:T(8,128)S(1)}, f32[6,32]{1,0:T(8,128)}, u32[]{:S(2)}) copy-start(f32[6,32]{1,0:T(8,128)} %param.46) | copy-start | bytes 2308
  1181.3 52.6 %copy-start.54 = (f32[6,32]{1,0:T(8,128)S(1)}, f32[6,32]{1,0:T(8,128)}, u32[]{:S(2)}) copy-start(f32[6,32]{1,0:T(8,128)} %param.53) | copy-start | bytes 2308
  1181.3 115.6 %copy-start.40 = (f32[64,32]{0,1:T(8,128)S(1)}, f32[64,32]{0,1:T(8,128)}, u32[]{:S(2)}) copy-start(f32[64,32]{0,1:T(8,128)} %param.36) | copy-start | bytes 24580
  1181.4 115.6 %copy-start.43 = (f32[64,32]{0,1:T(8,128)S(1)}, f32[64,32]{0,1:T(8,128)}, u32[]{:S(2)}) copy-start(f32[64,32]{0,1:T(8,128)} %param.43) | copy-start | bytes 24580
  1181.4 115.6 %copy-start.44 = (f32[64,32]{0,1:T(8,128)S(1)}, f32[64,32]{0,1:T(8,128)}, u32[]{:S(2)}) copy-start(f32[64,32]{0,1:T(8,128)} %param.50) | copy-start | bytes 24580
  1181.4 191.3 %copy-start.35 = (f32[3,32,64]{2,1,0:T(8,128)S(1)}, f32[3,32,64]{2,1,0:T(8,128)}, u32[]{:S(2)}) copy-start(f32[3,32,64]{2,1,0:T(8,128)} %param.35) | copy-start | bytes 73732
  1181.4 191.3 %copy-start.41 = (f32[3,32,64]{2,1,0:T(8,128)S(1)}, f32[3,32,64]{2,1,0:T(8,128)}, u32[]{:S(2)}) copy-start(f32[3,32,64]{2,1,0:T(8,128)} %param.42) | copy-start | bytes 73732
  1181.4 191.3 %copy-start.42 = (f32[3,32,64]{2,1,0:T(8,128)S(1)}, f32[3,32,64]{2,1,0:T(8,128)}, u32[]{:S(2)}) copy-start(f32[3,32,64]{2,1,0:T(8,128)} %param.49) | copy-start | bytes 73732
  1233.9 254.1 %copy-start.45 = (f32[6,32]{1,0:T(8,128)}, f32[6,32]{1,0:T(8,128)S(1)}, u32[]{:S(2)}) copy-start(f32[6,32]{1,0:T(8,128)S(1)} %copy.106) | copy-start | bytes 2308
  (70 other events, 326.4 us)
Sparse Core Ops, SparseCore 0:
  256.9 103.2 all-gather.10
  406.8 103.2 all-gather.12
  548.2 105.9 all-gather.14
  657.9 61.8 reduce-scatter.11
  724.0 60.9 reduce-scatter.9
  1172.3 60.8 reduce-scatter.13
  1237.0 59.8 reduce-scatter.7
  1300.3 71.4 all-reduce.6
  1373.4 105.1 all-gather.16
